TPU v7x, 128 devices: a whole 4x4x4 slice. The times are simulated.
128 devices in a mesh: sq: 128 (over x, z, y, core).
Axes of the slice: x: 4, y: 4, z: 4, core: 2. Of those that a mesh axis runs over, the one named last changes fastest.
Arguments:
- tokens: bfloat16 [4096, 2880], P('sq'), may hold values from -6 to 6
- norm_gain: float32 [2880], replicated, may hold values from 0.25 to 1.75
- expert_ids: int32 [4096, 4], P('sq'), may hold values from 0 to 31, all different within a row; in each aligned block of 32 rows (0 to 31, 32 to 63, ...) at most 5 rows name the same one
- combine_weight: float32 [4096, 4], P('sq'), may hold values from 0.05 to 0.6
- cotangent: bfloat16 [4096, 2880], P('sq'), may hold values from -6 to 6
- w_gate: bfloat16 [128, 2880, 720], P('sq'), may hold values from -0.109375 to 0.109375
- w_up: bfloat16 [128, 2880, 720], P('sq'), may hold values from -0.109375 to 0.109375
- w_down: bfloat16 [128, 720, 2880], P('sq'), may hold values from -0.109375 to 0.109375
Outputs:
- d_tokens: bfloat16 [4096, 2880], P('sq')
- grad_gate: bfloat16 [128, 2880, 720], P('sq')
- grad_up: bfloat16 [128, 2880, 720], P('sq')
- grad_down: bfloat16 [128, 720, 2880], P('sq')
Inputs may be any that keep to these rules, and one draw needn't show every extreme that they name: `expert_ids`: each row names 4 different experts; the rows of one device name any one expert at most 5 times, a bound that some block reaches.
All inputs are finite; a program needn't handle non-finite values.
Results may differ from a plain program's by a relative error of at most 0.0078.
Values may be sent and summed in bfloat16 or wider, within the bound.
A program may use at most 128 MiB of HBM per device.

v0:
```python
import jax
import jax.numpy as jnp
from jax import lax
from jax.sharding import PartitionSpec as P

QUARTERS = 4


norm_eps = 1e-05
glu_alpha = 1.702


def contract_rows(left, right):
    return lax.dot_general(
        left, right, (((0,), (0,)), ((), ())), preferred_element_type=jnp.float32
    )


def contract_cols(left, right):
    return lax.dot_general(
        left, right, (((1,), (1,)), ((), ())), preferred_element_type=jnp.float32
    )


def local(tokens, norm_gain, expert_ids, combine_weight, cotangent, w_gate, w_up, w_down):
    devices = lax.axis_size("sq")
    tok_count, top_count = expert_ids.shape
    width = tokens.shape[1]
    expert_count = devices // QUARTERS
    slot_count = tok_count * top_count * QUARTERS // devices + 1
    pick_count = tok_count * top_count
    expert_slots = expert_count * slot_count
    token_f = tokens.astype(jnp.float32)
    rstd = lax.rsqrt(jnp.mean(token_f * token_f, axis=-1, keepdims=True) + norm_eps)
    normed = (token_f * rstd * norm_gain).astype(jnp.bfloat16)
    flat_ids = expert_ids.reshape(pick_count)
    onehot = (flat_ids[:, None] == jnp.arange(expert_count, dtype=jnp.int32)[None, :]).astype(
        jnp.float32
    )
    row_iota = lax.broadcasted_iota(jnp.int32, (pick_count, pick_count), 0)
    col_iota = lax.broadcasted_iota(jnp.int32, (pick_count, pick_count), 1)
    lower = (row_iota > col_iota).astype(jnp.float32)
    earlier = jnp.dot(lower, onehot, preferred_element_type=jnp.float32)
    slot = jnp.sum(earlier * onehot, axis=-1).astype(jnp.int32)
    position = flat_ids * slot_count + slot
    select = (position[:, None] == jnp.arange(expert_slots, dtype=jnp.int32)[None, :]).astype(
        jnp.float32
    )
    select = select.reshape(tok_count, top_count, expert_slots)
    token_select = jnp.sum(select, axis=1)
    weight_select = jnp.sum(select * combine_weight[:, :, None], axis=1)
    send_x = contract_rows(token_select.astype(jnp.bfloat16), normed).astype(jnp.bfloat16)
    send_dy = lax.dot_general(
        weight_select,
        cotangent.astype(jnp.float32),
        (((0,), (0,)), ((), ())),
        precision=lax.Precision.HIGHEST,
        preferred_element_type=jnp.float32,
    ).astype(jnp.bfloat16)
    rows_total = devices * slot_count

    def spread(buffer):
        shaped = buffer.reshape(expert_count, 1, slot_count, width)
        return jnp.broadcast_to(shaped, (expert_count, QUARTERS, slot_count, width)).reshape(
            devices, slot_count, width
        )

    got_x, got_dy = (
        lax.all_to_all(spread(send_x), "sq", split_axis=0, concat_axis=0, tiled=True),
        lax.all_to_all(spread(send_dy), "sq", split_axis=0, concat_axis=0, tiled=True),
    )
    x_in = got_x.reshape(rows_total, width)
    dy_e = got_dy.reshape(rows_total, width)
    gate_w = w_gate[0]
    up_w = w_up[0]
    down_w = w_down[0]
    gate = jnp.dot(x_in, gate_w, preferred_element_type=jnp.float32)
    up = jnp.dot(x_in, up_w, preferred_element_type=jnp.float32)
    sig = jax.nn.sigmoid(glu_alpha * gate)
    glu = gate * sig
    hid = (glu * (up + 1.0)).astype(jnp.bfloat16)
    d_hid = contract_cols(dy_e, down_w)
    d_up = (d_hid * glu).astype(jnp.bfloat16)
    d_gate = (d_hid * (up + 1.0) * (sig + glu_alpha * gate * sig * (1.0 - sig))).astype(
        jnp.bfloat16
    )
    partial_rows = (contract_cols(d_gate, gate_w) + contract_cols(d_up, up_w)).astype(jnp.bfloat16)
    grad_gate = contract_rows(x_in, d_gate).astype(jnp.bfloat16)[None]
    grad_up = contract_rows(x_in, d_up).astype(jnp.bfloat16)[None]
    grad_down = contract_rows(hid, dy_e).astype(jnp.bfloat16)[None]
    back = lax.all_to_all(
        partial_rows.reshape(devices, slot_count, width),
        "sq",
        split_axis=0,
        concat_axis=0,
        tiled=True,
    )
    summed = jnp.sum(
        back.reshape(expert_count, QUARTERS, slot_count, width).astype(jnp.float32), axis=1
    )
    d_rows = summed.astype(jnp.bfloat16).reshape(expert_slots, width)
    d_normed = jnp.dot(
        token_select.astype(jnp.bfloat16), d_rows, preferred_element_type=jnp.float32
    )
    scaled = d_normed * norm_gain
    mixed = jnp.mean(token_f * scaled, axis=-1, keepdims=True)
    d_tokens = (rstd * scaled - token_f * rstd * rstd * rstd * mixed).astype(jnp.bfloat16)
    return (d_tokens, grad_gate, grad_up, grad_down)


def solution(mesh):
    placed = (
        P("sq", None),
        P(),
        P("sq", None),
        P("sq", None),
        P("sq", None),
        P("sq", None, None),
        P("sq", None, None),
        P("sq", None, None),
    )
    return jax.shard_map(
        local,
        mesh=mesh,
        in_specs=placed,
        out_specs=(P("sq", None), P("sq", None, None), P("sq", None, None), P("sq", None, None)),
        check_vma=False,
    )
```

profile of v0, /device:TPU:1, one launch (start us, length us, event | category | flops | bytes accessed | tf_op | source)
XLA Modules:
  0.0 307.5 jit_solution(15066598215991799202)
XLA Ops:
  0.6 0.0 copy-start
  0.6 1.1 fusion.22
  1.8 0.8 copy.26
  2.5 0.1 eq.29
  2.6 0.2 fusion.13
  2.8 0.1 convert_element_type.61
  2.9 0.1 copy.27
  3.0 0.7 multiply_add_fusion
  3.7 0.8 convert_reduce_fusion
  4.5 1.4 convolution_convert_fusion.3
  5.9 0.4 broadcast_in_dim.16
  6.4 3.0 broadcast_in_dim.34
  9.3 11.9 %all-to-all-start.1 = ((bf16[128,5,2880]{2,1,0:T(8,128)(2,1)}), bf16[128,5,2880]{2,1,0:T(8,128)(2,1)}, u32[]{:S(2)}, u32[]{:S(2)}) async-start(bf16[128,5,2880]{2,1,0:T(8,128)(2,1)} %bitcast.40), calls=%async_computation.1 | async-start | bytes 12058624 | tf_op jit(solution)/shard_map/all_to_all | solution.py:69
  21.2 0.0 copy-done
  21.2 0.9 convolution_convert_fusion.4
  22.2 0.4 broadcast_in_dim.14
  22.6 71.4 %all-to-all-done.1 = bf16[128,5,2880]{2,1,0:T(8,128)(2,1)} async-done(((bf16[128,5,2880]{2,1,0:T(8,128)(2,1)}), bf16[128,5,2880]{2,1,0:T(8,128)(2,1)}, u32[]{:S(2)}, u32[]{:S(2)}) %all-to-all-start.1) | async-done | bytes 3686432 | tf_op jit(solution)/shard_map/all_to_all | solution.py:69
  94.0 3.0 broadcast_in_dim.15
  97.0 8.4 %all-to-all-start = ((bf16[128,5,2880]{2,1,0:T(8,128)(2,1)}), bf16[128,5,2880]{2,1,0:T(8,128)(2,1)}, u32[]{:S(2)}, u32[]{:S(2)}) async-start(bf16[128,5,2880]{2,1,0:T(8,128)(2,1)} %bitcast.41), calls=%async_computation | async-start | bytes 12058624 | tf_op jit(solution)/shard_map/all_to_all | solution.py:70
  105.4 0.0 slice-start.2
  105.4 7.9 %reshape.71 = bf16[640,2880]{1,0:T(8,128)(2,1)} reshape(bf16[128,5,2880]{2,1,0:T(8,128)(2,1)} %all-to-all-done.1) | data formatting | bytes 7372800 | tf_op jit(solution)/shard_map/reshape | solution.py:72
  113.4 0.0 copy-start.2
  113.4 0.0 slice-start.3
  113.4 8.3 %fusion.5 = f32[640,720]{0,1:T(8,128)} fusion(bf16[640,2880]{1,0:T(8,128)(2,1)} %reshape.71, bf16[1,2880,720]{1,2,0:T(8,128)(2,1)} %param.13), kind=kOutput, calls=%fused_computation.10 | convolution fusion | flops 2654208000 | bytes 9676800 | tf_op jit(solution)/shard_map/dot_general | solution.py:77
  121.7 0.0 slice-done.2
  121.7 0.0 copy-done.2
  121.7 0.0 slice-done.3
  121.8 4.9 %fusion.8 = f32[640,720]{0,1:T(8,128)} fusion(bf16[640,2880]{1,0:T(8,128)(2,1)S(1)} %copy-done.2, bf16[1,2880,720]{1,2,0:T(8,128)(2,1)S(1)} %bitcast.45), kind=kOutput, calls=%fused_computation.13 | convolution fusion | flops 2654208000 | bytes 9676800 | tf_op jit(solution)/shard_map/dot_general | solution.py:78
  126.6 51.6 %all-to-all-done = bf16[128,5,2880]{2,1,0:T(8,128)(2,1)} async-done(((bf16[128,5,2880]{2,1,0:T(8,128)(2,1)}), bf16[128,5,2880]{2,1,0:T(8,128)(2,1)}, u32[]{:S(2)}, u32[]{:S(2)}) %all-to-all-start) | async-done | bytes 3686432 | tf_op jit(solution)/shard_map/all_to_all | solution.py:70
  178.2 0.0 slice-start
  178.2 8.0 %reshape.69 = bf16[640,2880]{1,0:T(8,128)(2,1)} reshape(bf16[128,5,2880]{2,1,0:T(8,128)(2,1)} %all-to-all-done) | data formatting | bytes 7372800 | tf_op jit(solution)/shard_map/reshape | solution.py:73
  186.3 0.0 slice-start.1
  186.3 8.6 %multiply_convert_fusion.1 = (bf16[640,720]{0,1:T(8,128)(2,1)S(1)}, bf16[640,720]{0,1:T(8,128)(2,1)S(1)}) fusion(f32[640,720]{0,1:T(8,128)} %fusion.5, f32[640,720]{0,1:T(8,128)} %fusion.8, bf16[640,2880]{1,0:T(8,128)(2,1)} %reshape.69, bf16[1,720,2880]{2,1,0:T(8,128)(2,1)} %param.15), kind=kOutput, calls=%fused_computation.21 | convolution fusion | flops 2661120000 | bytes 13363200 | tf_op jit(solution)/shard_map/dot_general | solution.py:20
  194.8 0.0 slice-done
  194.8 0.0 slice-done.1
  194.8 4.0 %fusion.3 = f32[640,2880]{0,1:T(8,128)S(1)} fusion(bf16[640,720]{0,1:T(8,128)(2,1)S(1)} %get-tuple-element.7, bf16[1,2880,720]{1,2,0:T(8,128)(2,1)S(1)} %bitcast.43), kind=kOutput, calls=%fused_computation.8 | convolution fusion | flops 2654208000 | bytes 12441600 | tf_op jit(solution)/shard_map/dot_general | solution.py:20
  198.9 8.0 %add_convert_fusion = bf16[640,2880]{0,1:T(8,128)(2,1)} fusion(f32[640,2880]{0,1:T(8,128)S(1)} %fusion.3, bf16[640,720]{0,1:T(8,128)(2,1)S(1)} %get-tuple-element.6, bf16[1,2880,720]{1,2,0:T(8,128)(2,1)} %param.14), kind=kOutput, calls=%fused_computation | convolution fusion | flops 2657894400 | bytes 16128000 | tf_op jit(solution)/shard_map/dot_general | solution.py:20
  206.9 6.2 %copy.28 = bf16[640,2880]{1,0:T(8,128)(2,1)} copy(bf16[640,2880]{0,1:T(8,128)(2,1)} %add_convert_fusion) | data formatting | bytes 7372800 | tf_op jit(solution)/shard_map/convert_element_type | solution.py:87
  213.0 7.3 %reshape.72 = bf16[128,5,2880]{2,1,0:T(8,128)(2,1)} reshape(bf16[640,2880]{1,0:T(8,128)(2,1)} %copy.28) | data formatting | bytes 7372800 | tf_op jit(solution)/shard_map/reshape | solution.py:92
  220.4 8.4 %all-to-all-start.2 = ((bf16[128,5,2880]{2,1,0:T(8,128)(2,1)}), bf16[128,5,2880]{2,1,0:T(8,128)(2,1)}, u32[]{:S(2)}, u32[]{:S(2)}) async-start(bf16[128,5,2880]{2,1,0:T(8,128)(2,1)} %reshape.72), calls=%async_computation.2 | async-start | bytes 12058624 | tf_op jit(solution)/shard_map/all_to_all | solution.py:91
  228.8 0.0 copy-start.3
  228.8 7.4 %fusion.2 = bf16[1,2880,720]{1,2,0:T(8,128)(2,1)} fusion(bf16[640,720]{0,1:T(8,128)(2,1)S(1)} %get-tuple-element.6, bf16[640,2880]{1,0:T(8,128)(2,1)} %reshape.71), kind=kOutput, calls=%fused_computation.7 | convolution fusion | flops 2656281600 | bytes 8755200 | tf_op jit(solution)/shard_map/dot_general | solution.py:14
  236.1 0.0 copy-done.3
  236.1 0.0 copy-start.4
  236.1 0.0 copy-start.7
  236.1 0.0 copy-start.8
  236.2 5.2 %fusion.1 = bf16[1,2880,720]{1,2,0:T(8,128)(2,1)} fusion(bf16[640,720]{0,1:T(8,128)(2,1)S(1)} %get-tuple-element.7, bf16[640,2880]{1,0:T(8,128)(2,1)S(1)} %copy-done.3), kind=kOutput, calls=%fused_computation.6 | convolution fusion | flops 2656281600 | bytes 8755200 | tf_op jit(solution)/shard_map/dot_general | solution.py:14
  241.3 0.0 copy-done.4
  241.3 0.0 copy-done.7
  241.3 0.0 copy-done.8
  241.3 5.3 %fusion = bf16[1,720,2880]{2,1,0:T(8,128)(2,1)} fusion(bf16[640,2880]{1,0:T(8,128)(2,1)S(1)} %copy-done.4, f32[640,720]{0,1:T(8,128)S(1)} %copy-done.8, f32[640,720]{0,1:T(8,128)S(1)} %copy-done.7), kind=kOutput, calls=%fused_computation.5 | convolution fusion | flops 2659968000 | bytes 11520000 | tf_op jit(solution)/shard_map/dot_general | solution.py:14
  246.6 0.0 copy-start.5
  246.6 0.0 copy-start.6
  246.6 54.9 %all-to-all-done.2 = bf16[128,5,2880]{2,1,0:T(8,128)(2,1)} async-done(((bf16[128,5,2880]{2,1,0:T(8,128)(2,1)}), bf16[128,5,2880]{2,1,0:T(8,128)(2,1)}, u32[]{:S(2)}, u32[]{:S(2)}) %all-to-all-start.2) | async-done | bytes 3686432 | tf_op jit(solution)/shard_map/all_to_all | solution.py:91
  301.6 0.0 copy-start.1
  301.6 4.0 %bitcast_reduce_fusion = bf16[32,5,2880]{2,1,0:T(8,128)(2,1)S(1)} fusion(bf16[128,5,2880]{2,1,0:T(8,128)(2,1)} %all-to-all-done.2), kind=kLoop, calls=%fused_computation.1 | loop fusion | flops 1382400 | bytes 4608000 | tf_op jit(solution)/shard_map/reduce_sum | solution.py:98
  305.5 0.7 reshape.74
  306.2 0.0 copy-done.5
  306.3 0.0 copy-done.6
  306.3 0.4 fusion.23
  306.7 0.8 fusion.21
  307.5 0.0 copy-done.1
  (5 shorter events, 0.0 us)
Async XLA Ops:
  0.6 20.6 %copy-start = (bf16[32,2880]{1,0:T(8,128)(2,1)S(1)}, bf16[32,2880]{1,0:T(8,128)(2,1)}, u32[]{:S(2)}) copy-start(bf16[32,2880]{1,0:T(8,128)(2,1)} %param.12) | copy-start | bytes 552964
  9.3 84.7 %all-to-all-start.1 = ((bf16[128,5,2880]{2,1,0:T(8,128)(2,1)}), bf16[128,5,2880]{2,1,0:T(8,128)(2,1)}, u32[]{:S(2)}, u32[]{:S(2)}) async-start(bf16[128,5,2880]{2,1,0:T(8,128)(2,1)} %bitcast.40), calls=%async_computation.1 | async-start | bytes 12058624 | tf_op jit(solution)/shard_map/all_to_all | solution.py:69
  97.0 81.2 %all-to-all-start = ((bf16[128,5,2880]{2,1,0:T(8,128)(2,1)}), bf16[128,5,2880]{2,1,0:T(8,128)(2,1)}, u32[]{:S(2)}, u32[]{:S(2)}) async-start(bf16[128,5,2880]{2,1,0:T(8,128)(2,1)} %bitcast.41), calls=%async_computation | async-start | bytes 12058624 | tf_op jit(solution)/shard_map/all_to_all | solution.py:70
  105.4 16.3 %slice-start.2 = ((s8[4239360]{0:T(1024)(128)(4,1)}), s8[45056]{0:T(1024)(128)(4,1)S(1)}, s32[]{:S(2)}) async-start(s8[4239360]{0:T(1024)(128)(4,1)} %bitcast.44), calls=%async_computation.5 | async-start | bytes 90112
  113.4 8.4 %copy-start.2 = (bf16[640,2880]{1,0:T(8,128)(2,1)S(1)}, bf16[640,2880]{1,0:T(8,128)(2,1)}, u32[]{:S(2)}) copy-start(bf16[640,2880]{1,0:T(8,128)(2,1)} %reshape.71) | copy-start | bytes 11059204
  113.4 8.4 %slice-start.3 = ((s8[4239360]{0:T(1024)(128)(4,1)}), s8[4194304]{0:T(1024)(128)(4,1)S(1)}, s32[]{:S(2)}) async-start(s8[4239360]{0:T(1024)(128)(4,1)} %bitcast.44), calls=%async_computation.6 | async-start | bytes 8388608
  178.2 16.6 %slice-start = ((s8[4239360]{0:T(1024)(128)(4,1)}), s8[45056]{0:T(1024)(128)(4,1)S(1)}, s32[]{:S(2)}) async-start(s8[4239360]{0:T(1024)(128)(4,1)} %bitcast.42), calls=%async_computation.3 | async-start | bytes 90112
  186.3 8.6 %slice-start.1 = ((s8[4239360]{0:T(1024)(128)(4,1)}), s8[4194304]{0:T(1024)(128)(4,1)S(1)}, s32[]{:S(2)}) async-start(s8[4239360]{0:T(1024)(128)(4,1)} %bitcast.42), calls=%async_computation.4 | async-start | bytes 8388608
  220.4 81.2 %all-to-all-start.2 = ((bf16[128,5,2880]{2,1,0:T(8,128)(2,1)}), bf16[128,5,2880]{2,1,0:T(8,128)(2,1)}, u32[]{:S(2)}, u32[]{:S(2)}) async-start(bf16[128,5,2880]{2,1,0:T(8,128)(2,1)} %reshape.72), calls=%async_computation.2 | async-start | bytes 12058624 | tf_op jit(solution)/shard_map/all_to_all | solution.py:91
  228.8 7.4 %copy-start.3 = (bf16[640,2880]{1,0:T(8,128)(2,1)S(1)}, bf16[640,2880]{1,0:T(8,128)(2,1)}, u32[]{:S(2)}) copy-start(bf16[640,2880]{1,0:T(8,128)(2,1)} %reshape.71) | copy-start | bytes 11059204
  236.1 5.2 %copy-start.4 = (bf16[640,2880]{1,0:T(8,128)(2,1)S(1)}, bf16[640,2880]{1,0:T(8,128)(2,1)}, u32[]{:S(2)}) copy-start(bf16[640,2880]{1,0:T(8,128)(2,1)} %reshape.69) | copy-start | bytes 11059204
  236.1 5.2 %copy-start.7 = (f32[640,720]{0,1:T(8,128)S(1)}, f32[640,720]{0,1:T(8,128)}, u32[]{:S(2)}) copy-start(f32[640,720]{0,1:T(8,128)} %fusion.5) | copy-start | bytes 5529604
  236.1 5.2 %copy-start.8 = (f32[640,720]{0,1:T(8,128)S(1)}, f32[640,720]{0,1:T(8,128)}, u32[]{:S(2)}) copy-start(f32[640,720]{0,1:T(8,128)} %fusion.8) | copy-start | bytes 5529604
  246.6 59.6 %copy-start.5 = (bf16[32,2880]{1,0:T(8,128)(2,1)S(1)}, bf16[32,2880]{1,0:T(8,128)(2,1)}, u32[]{:S(2)}) copy-start(bf16[32,2880]{1,0:T(8,128)(2,1)} %param.8) | copy-start | bytes 552964
  246.6 59.6 %copy-start.6 = (f32[2880]{0:T(1024)S(1)}, f32[2880]{0:T(1024)}, u32[]{:S(2)}) copy-start(f32[2880]{0:T(1024)} %param.9) | copy-start | bytes 34564
  301.6 6.0 %copy-start.1 = (bf16[32,2880]{1,0:T(8,128)(2,1)S(1)}, bf16[32,2880]{1,0:T(8,128)(2,1)}, u32[]{:S(2)}) copy-start(bf16[32,2880]{1,0:T(8,128)(2,1)} %param.12) | copy-start | bytes 552964
where the time goes:
time: 309 us; the launch traced here: 308 us
  waiting for transfers between devices  178 us (58%)
  matrix products  54.5 us (18%)
  local copies, waits for them, and re-layouts  38.1 us (12%)
  starting transfers between devices  28.7 us (9%)
  other arithmetic  7.43 us (2%)
    all_to_all x1, waiting for transfers between devices, local(): lax.all_to_all(spread(send_x), 'sq', split_axis=0, concat_axis=0, tiled=T...  71.4 us
    all_to_all x1, waiting for transfers between devices, local(): lax.all_to_all(partial_rows.reshape(devices, slot_count, width), 'sq', sp...  54.9 us
    all_to_all x1, waiting for transfers between devices, local(): lax.all_to_all(spread(send_dy), 'sq', split_axis=0, concat_axis=0, tiled=...  51.6 us
    dot_general x3, matrix products, contract_cols(): lax.dot_general(left, right, (((1,), (1,)), ((), ())), preferred_element_...  20.6 us
    dot_general x4, matrix products, contract_rows(): lax.dot_general(left, right, (((0,), (0,)), ((), ())), preferred_element_...  19.2 us
    all_to_all x1, starting transfers between devices, local(): lax.all_to_all(spread(send_x), 'sq', split_axis=0, concat_axis=0, tiled=T...  11.9 us
    all_to_all x1, starting transfers between devices, local(): lax.all_to_all(partial_rows.reshape(devices, slot_count, width), 'sq', sp...  8.42 us
    all_to_all x1, starting transfers between devices, local(): lax.all_to_all(spread(send_dy), 'sq', split_axis=0, concat_axis=0, tiled=...  8.41 us
  transfers between devices with their start and end apart: 3, of which 3 were waited for; matrix products, arithmetic and copies ran while one was open for 13% of the time, Pallas kernels for 0%

commit v1 on v0

v1 whole, which is shorter than its diff:
```python
import functools

import jax
import jax.numpy as jnp
from jax import lax
from jax.experimental import pallas as pl
from jax.experimental.pallas import tpu as pltpu
from jax.sharding import PartitionSpec as P

MESH = pl.DeviceIdType.MESH
BF = jnp.bfloat16
F32 = jnp.float32

eps = 1e-05
alpha = 1.702

D = 2880
FQ = 720
TOK = 32
TOP = 4
SLOTS = 5
CW = 768
HW = CW // 2
NK = -(-D // CW)
VALID = [min(CW, D - k * CW) for k in range(NK)]
LANES = [-(-v // 128) * 128 for v in VALID]
EARLY = [False, False, False, False]
ROWS = 8 * SLOTS
BLK = 4 * ROWS
TOTAL = 4 * BLK
NG = 3
GB = FQ // NG


def dot(a, b):
    return jnp.dot(a, b, preferred_element_type=F32)


def dot_t(a, b):
    return lax.dot_general(a, b, (((1,), (1,)), ((), ())), preferred_element_type=F32)


def dot_0(a, b):
    return lax.dot_general(a, b, (((0,), (0,)), ((), ())), preferred_element_type=F32)


def device(x, z, y, c):
    return (((x * 4 + z) * 4 + y) * 2 + c,)


def kernel(
    tok_ref, gain_ref, ids_ref, cw_ref, cot_ref, wg_hbm, wu_hbm, wd_hbm,
    dtok_ref, gg_hbm, gu_hbm, gd_hbm,
    wg, wu, wd, own, meta_own, meta_got, gath, rows, xd, sel_f, sel, scale, up_a, gate_a, dhid_a,
    dg, du, dg_t, du_t, hid_t, part, part_got, psum, h_got, drow, z_got, tsum, x_got, f_out, f_got, dn, gs,
    wsem, psem, msem, msend, fsem, hsem, xsem, zsem, ysem, csem, rcsem, rhsem, rzsem, rxsem, rfsem,
    send, gsem,
):
    me = lax.axis_index("sq")
    c = lax.rem(me, 2)
    y = lax.rem(me // 2, 4)
    z = lax.rem(me // 8, 4)
    x = me // 32
    h = lax.rem(y, 2)
    half = y // 2
    yp = y + 1 - 2 * h
    yl = 3 - y
    any_early = any(EARLY)

    weights = [
        pltpu.make_async_copy(wg_hbm.at[0], wg, wsem.at[0]),
        pltpu.make_async_copy(wu_hbm.at[0], wu, wsem.at[1]),
        pltpu.make_async_copy(wd_hbm.at[0], wd, wsem.at[2]),
    ]
    for w in weights:
        w.start()

    peers_x = [(dx, dr) for dx in range(4) for dr in range(2) if (dx, dr) != (0, 0)]
    peers_z = [(dz, pr) for dz in range(4) for pr in range(2) if (dz, pr) != (0, 0)]

    def x_peer(dx, dr):
        return lax.rem(x + dx, 4), lax.rem(c + dr, 2)

    def z_peer(dz, pr):
        return lax.rem(z + dz, 4), (yl if pr else y)

    barrier = pltpu.get_barrier_semaphore()
    for p in peers_x:
        xx, cc = x_peer(*p)
        pl.semaphore_signal(barrier, inc=1, device_id=device(xx, z, y, cc), device_id_type=MESH)
    for p in peers_z:
        zz, yy = z_peer(*p)
        pl.semaphore_signal(barrier, inc=1, device_id=device(x, zz, yy, c), device_id_type=MESH)
    pl.semaphore_signal(barrier, inc=1, device_id=device(x, z, yp, c), device_id_type=MESH)

    def gain(lo, v):
        return gain_ref[pl.ds(lo, v)].reshape(1, v)

    tf = tok_ref[...].astype(F32)
    rstd = lax.rsqrt(jnp.mean(tf * tf, axis=-1, keepdims=True) + eps)
    for k in range(NK):
        lo, v, n = k * CW, VALID[k], LANES[k]
        if v < n:
            own[k, 0, h, :, :] = jnp.zeros((TOK, CW), BF)
            own[k, 1, h, :, :] = jnp.zeros((TOK, CW), BF)
        own[k, 0, h, :, 0:v] = (tf[:, lo : lo + v] * rstd * gain(lo, v)).astype(BF)
        own[k, 1, h, :, 0:v] = cot_ref[:, lo : lo + v]

    lane = lax.broadcasted_iota(jnp.int32, (TOK, 256), 1)
    trow = lax.broadcasted_iota(jnp.int32, (TOK, 256), 0)
    place = jnp.where(lane == trow + TOK * (2 * x + c), 1.0, 0.0).astype(BF)
    w_all = cw_ref[...]
    w_hi = w_all.astype(BF)
    w_rest = w_all - w_hi.astype(F32)
    w_mid = w_rest.astype(BF)
    w_lo = (w_rest - w_mid.astype(F32)).astype(BF)
    meta_own[h, 0:TOP, :] = dot(ids_ref[...].astype(F32).astype(BF), place)
    meta_own[h, TOP : 2 * TOP, :] = dot(w_hi, place) + dot(w_mid, place) + dot(w_lo, place)

    pl.semaphore_wait(barrier, len(peers_x) + len(peers_z) + 1)

    sends = []
    count = [0]

    def put(src, dst, recv, dev):
        cp = pltpu.make_async_remote_copy(
            src_ref=src, dst_ref=dst, send_sem=send.at[count[0]], recv_sem=recv,
            device_id=dev, device_id_type=MESH,
        )
        count[0] += 1
        cp.start()
        sends.append(cp)

    def arrived(dst, sem):
        pltpu.make_async_copy(dst, dst, sem).wait()

    src_mine = 2 * x + c

    for k in range(NK):
        if EARLY[k]:
            n = LANES[k]
            o = own.at[k, :, h, :, pl.ds(0, n)]
            put(o, o, fsem.at[k], device(x, z, yp, c))
    if any_early:
        put(meta_own.at[h], meta_own.at[h], fsem.at[NK], device(x, z, yp, c))

    def slabs(ref, index, row, count, n):
        return ref.at[(*index, pl.ds(row // 8, count // 8), slice(None), pl.ds(0, n))]

    def flat(ref, *index):
        r = ref.at[index]
        return r.reshape(r.shape[0] * 8, r.shape[2])

    def send_x(k):
        n = LANES[k]
        hs = [0, 1] if EARLY[k] else [h]
        if EARLY[k]:
            o = own.at[k, :, 1 - h, :, pl.ds(0, n)]
            arrived(o, fsem.at[k])
        for i, hh in enumerate(hs):
            for p in peers_x:
                xx, cc = x_peer(*p)
                put(
                    own.at[k, cc, hh, :, pl.ds(0, n)],
                    gath.at[k, hh, pl.ds(TOK * src_mine, TOK), pl.ds(0, n)],
                    xsem.at[k, i, src_mine],
                    device(xx, z, y, cc),
                )
            pltpu.make_async_copy(
                own.at[k, c, hh, :, pl.ds(0, n)],
                gath.at[k, hh, pl.ds(TOK * src_mine, TOK), pl.ds(0, n)],
                xsem.at[k, i, src_mine],
            ).start()

    hs_meta = [0, 1] if any_early else [h]

    def send_meta():
        if any_early:
            arrived(meta_own.at[1 - h], fsem.at[NK])
        for i, hh in enumerate(hs_meta):
            for p in peers_x:
                xx, cc = x_peer(*p)
                put(
                    meta_own.at[hh], meta_got.at[hh, src_mine], msem.at[i, src_mine],
                    device(xx, z, y, cc),
                )
            pltpu.make_async_copy(
                meta_own.at[hh], meta_got.at[hh, src_mine], msem.at[i, src_mine]
            ).start()

    late = [k for k in range(NK) if not EARLY[k]]
    order = list(range(NK))
    if not any_early:
        send_meta()
        for k in order:
            send_x(k)
    else:
        for k in late[:1]:
            send_x(k)
        send_meta()
        for k in order:
            if k not in late[:1]:
                send_x(k)

    def build():
        e_of = lax.broadcasted_iota(jnp.int32, (8, 256), 0).astype(F32) + (8 * x).astype(F32)
        t1 = lax.broadcasted_iota(jnp.int32, (256, 256), 0)
        t2 = lax.broadcasted_iota(jnp.int32, (256, 256), 1)
        lower = jnp.where((t1 < t2) & (t1 // TOK == t2 // TOK), 1.0, 0.0).astype(BF)
        r = lax.broadcasted_iota(jnp.int32, (ROWS, 256), 0)
        t = lax.broadcasted_iota(jnp.int32, (ROWS, 256), 1)
        src_ok = r // SLOTS == t // TOK
        slot_of = lax.rem(r, SLOTS).astype(F32)
        for i, hh in enumerate(hs_meta):
            for s in range(8):
                arrived(meta_got.at[hh, s], msem.at[i, s])
            meta = meta_got[hh, 0]
            for s in range(1, 8):
                meta = meta + meta_got[hh, s]
            named = jnp.zeros((8, 256), F32)
            weight = jnp.zeros((8, 256), F32)
            for j in range(TOP):
                hit = meta[j : j + 1, :] == e_of
                named = named + jnp.where(hit, 1.0, 0.0)
                weight = weight + jnp.where(hit, meta[TOP + j : TOP + j + 1, :], 0.0)
            rank = dot(named.astype(BF), lower)
            for e in range(8):
                on = src_ok & (rank[e : e + 1, :] == slot_of)
                one = jnp.where(on, jnp.broadcast_to(named[e : e + 1, :], (ROWS, 256)), 0.0)
                sel_f[pl.ds(e * ROWS, ROWS), :] = one
                w_row = jnp.sum(one * weight[e : e + 1, :], axis=-1, keepdims=True)
                scale[hh, pl.ds(e * ROWS, ROWS), :] = jnp.broadcast_to(
                    jnp.where(c == 0, jnp.ones_like(w_row), w_row), (ROWS, 128)
                )
            sel[hh, :, :] = sel_f[...].astype(BF)

    def select(k):
        n = LANES[k]
        hs = [0, 1] if EARLY[k] else [h]
        for i, hh in enumerate(hs):
            for s in range(8):
                arrived(gath.at[k, hh, pl.ds(TOK * s, TOK), pl.ds(0, n)], xsem.at[k, i, s])
        for i, hh in enumerate(hs):
            picked = dot(sel[hh], gath[k, hh, :, 0:n])
            picked = (picked * scale[hh, :, 0:1]).astype(BF)
            flat(rows, k, hh)[:, 0:n] = picked
            ys = 2 * half + hh if EARLY[k] else y
            for dz in range(4):
                for pr in range(2):
                    zz, yy = z_peer(dz, pr)
                    pp = half + pr * (1 - 2 * half)
                    src = slabs(rows, (k, hh), (zz * 2 + pp) * ROWS, ROWS, n)
                    dst = slabs(xd, (k, c), ys * BLK + z * ROWS, ROWS, n)
                    sem = zsem.at[k, i, pr, z]
                    if dz == 0 and pr == 0:
                        pltpu.make_async_copy(src, dst, sem).start()
                    else:
                        put(src, dst, sem, device(x, zz, yy, c))

    def block(k, ys):
        return slabs(xd, (k, c), ys * BLK, BLK, LANES[k])

    def wait_z(k, i, pr, ys):
        n = LANES[k]
        for s in range(4):
            arrived(slabs(xd, (k, c), ys * BLK + s * ROWS, ROWS, n), zsem.at[k, i, pr, s])

    def to_core(k, ys):
        put(block(k, ys), block(k, ys), csem.at[k, ys], device(x, z, y, 1 - c))

    def forward(k):
        if EARLY[k]:
            for pr in range(2):
                for i in range(2):
                    ys = 2 * (half + pr * (1 - 2 * half)) + i
                    wait_z(k, i, pr, ys)
                    to_core(k, ys)
        else:
            for pr, ys in enumerate((y, yl)):
                wait_z(k, 0, pr, ys)
                put(block(k, ys), block(k, ys), ysem.at[k, pr], device(x, z, yp, c))
                to_core(k, ys)

    def finish(k):
        if not EARLY[k]:
            for pr, ys in enumerate((yp, 3 - yp)):
                arrived(block(k, ys), ysem.at[k, pr])
                to_core(k, ys)

    def up_matmuls(k):
        n, v, lo = LANES[k], VALID[k], k * CW
        for ys in range(4):
            arrived(slabs(xd, (k, 1 - c), ys * BLK, BLK, n), csem.at[k, ys])
        if k == 0:
            for w in weights:
                w.wait()
        xs = flat(xd, k, 0)[:, 0:v]
        gate = dot_t(xs, wg[:, lo : lo + v])
        gate_a[...] = gate if k == 0 else gate_a[...] + gate
        up = dot_t(xs, wu[:, lo : lo + v])
        up_a[...] = up if k == 0 else up_a[...] + up
        dhid = dot_t(flat(xd, k, 1)[:, 0:v], wd[:, lo : lo + v])
        dhid_a[...] = dhid if k == 0 else dhid_a[...] + dhid

    build()
    for step in range(NK + 3):
        if step < NK:
            select(step)
        if 0 <= step - 1 < NK:
            forward(step - 1)
        if 0 <= step - 2 < NK:
            finish(step - 2)
        if 0 <= step - 3 < NK:
            up_matmuls(step - 3)

    def pointwise(i, carry):
        b = pl.ds(pl.multiple_of(i * BLK, BLK), BLK)
        gate = gate_a[b, :]
        sig = jax.nn.sigmoid(alpha * gate)
        glu = gate * sig
        up1 = up_a[b, :] + 1.0
        gate_a[b, :] = glu * up1
        d_hid = dhid_a[b, :]
        du[b, :] = (d_hid * glu).astype(BF)
        dg[b, :] = (d_hid * up1 * (sig + alpha * gate * sig * (1.0 - sig))).astype(BF)
        return carry

    lax.fori_loop(0, 4, pointwise, 0)

    def partial(k):
        lo, v = k * CW, VALID[k]
        if v < CW:
            part[k, 1, :, :] = jnp.zeros((TOTAL, HW), BF)
        p = dot(dg[...], wg[:, lo : lo + v]) + dot(du[...], wu[:, lo : lo + v])
        p = p.astype(BF)
        part[k, 0, :, :] = p[:, 0:HW]
        part[k, 1, :, 0 : v - HW] = p[:, HW:v]
        put(part.at[k, 1 - c], part_got.at[k], rcsem.at[k], device(x, z, y, 1 - c))

    def back_z(k, src_ref, base_of):
        for pr in range(2):
            ydst = yl if pr else y
            his = [0, 1] if EARLY[k] else [0]
            for i in his:
                hd = i if EARLY[k] else lax.rem(ydst, 2)
                for dz in range(4):
                    zz = lax.rem(z + dz, 4)
                    src = slabs(src_ref, (k,), base_of(pr, i) * BLK + zz * ROWS, ROWS, HW)
                    dst = slabs(z_got, (k, hd), (z * 2 + half) * ROWS, ROWS, HW)
                    sem = rzsem.at[k, i, z * 2 + half]
                    if dz == 0 and pr == 0:
                        pltpu.make_async_copy(src, dst, sem).start()
                    else:
                        put(src, dst, sem, device(x, zz, ydst, c))

    def back_core(k):
        arrived(part_got.at[k], rcsem.at[k])
        flat(psum, k)[...] = (part[k, c].astype(F32) + part_got[k].astype(F32)).astype(BF)
        if EARLY[k]:
            back_z(k, psum, lambda pr, i: 2 * (half + pr * (1 - 2 * half)) + i)
        else:
            for j, ys in enumerate((yp, 3 - yp)):
                put(
                    slabs(psum, (k,), ys * BLK, BLK, HW), slabs(h_got, (k,), j * BLK, BLK, HW),
                    rhsem.at[k, j], device(x, z, yp, c),
                )

    def back_pair(k):
        if not EARLY[k]:
            for j, ys in enumerate((y, yl)):
                arrived(slabs(h_got, (k,), j * BLK, BLK, HW), rhsem.at[k, j])
                b = pl.ds(pl.multiple_of(ys * BLK, BLK), BLK)
                to = pl.ds(j * BLK, BLK)
                flat(drow, k)[to, :] = (
                    flat(psum, k)[b, :].astype(F32) + flat(h_got, k)[to, :].astype(F32)
                ).astype(BF)
            back_z(k, drow, lambda pr, i: pr)

    def back_token(k):
        hs = [0, 1] if EARLY[k] else [h]
        for i, hh in enumerate(hs):
            for e in range(8):
                arrived(slabs(z_got, (k, hh), e * ROWS, ROWS, HW), rzsem.at[k, i, e])
        for i, hh in enumerate(hs):
            tsum[k, hh, :, :] = dot_0(sel[hh], flat(z_got, k, hh)[...]).astype(BF)
            for p in peers_x:
                xx, cc = x_peer(*p)
                put(
                    tsum.at[k, hh, pl.ds((2 * xx + cc) * TOK, TOK), :],
                    x_got.at[k, hh, src_mine],
                    rxsem.at[k, i, src_mine],
                    device(xx, z, y, cc),
                )
            pltpu.make_async_copy(
                tsum.at[k, hh, pl.ds(src_mine * TOK, TOK), :],
                x_got.at[k, hh, src_mine],
                rxsem.at[k, i, src_mine],
            ).start()

    def gather_sum(k, hh, r):
        s = x_got[k, hh, r].astype(F32)
        for j in range(1, 4):
            s = s + x_got[k, hh, 2 * j + r].astype(F32)
        return s

    def back_x(k):
        hs = [0, 1] if EARLY[k] else [h]
        for i, hh in enumerate(hs):
            for s in range(8):
                arrived(x_got.at[k, hh, s], rxsem.at[k, i, s])
        for r in range(2):
            dn[2 * k + r] = gather_sum(k, h, r)
        if EARLY[k]:
            for r in range(2):
                f_out[k, r] = gather_sum(k, 1 - h, r).astype(BF)
            put(f_out.at[k], f_got.at[k], rfsem.at[k], device(x, z, yp, c))

    def back_last(k):
        if EARLY[k]:
            arrived(f_got.at[k], rfsem.at[k])
            for r in range(2):
                dn[2 * k + r] = dn[2 * k + r] + f_got[k, r].astype(F32)

    stores = []

    def grad(which, b):
        slot = len(stores) % 2
        if len(stores) >= 2:
            stores[-2].wait()
        left = (dg_t, du_t, hid_t)[which]
        for k in range(NK):
            lo, v = k * CW, VALID[k]
            gs[slot, :, lo : lo + v] = dot(
                left[b * GB : (b + 1) * GB, :], flat(xd, k, which // 2)[:, 0:v]
            ).astype(BF)
        cp = pltpu.make_async_copy(
            gs.at[slot], (gg_hbm, gu_hbm, gd_hbm)[which].at[0, pl.ds(b * GB, GB), :],
            gsem.at[len(stores)],
        )
        cp.start()
        stores.append(cp)

    fill = [lambda w=w, b=b: grad(w, b) for w in range(3) for b in range(NG)]

    def filler():
        if fill:
            fill.pop(0)()

    for step in range(NK + 5):
        if step < NK:
            partial(step)
        if step == 0:
            hid_t[...] = gate_a[...].T.astype(BF)
            dg_t[...] = dg[...].T
            du_t[...] = du[...].T
        if 0 <= step - 1 < NK:
            back_core(step - 1)
        if 0 <= step - 2 < NK:
            back_pair(step - 2)
        if step >= 2:
            filler()
        if 0 <= step - 3 < NK:
            back_token(step - 3)
        if 0 <= step - 4 < NK:
            back_x(step - 4)
        if 0 <= step - 5 < NK:
            back_last(step - 5)
    while fill:
        filler()

    total = jnp.zeros((TOK, 1), F32)
    for k in range(NK):
        for r in range(2):
            lo = k * CW + r * HW
            v = max(0, min(HW, D - lo))
            if v:
                u = dn[2 * k + r, :, 0:v] * gain(lo, v)
                dn[2 * k + r, :, 0:v] = u
                total = total + jnp.sum(tf[:, lo : lo + v] * u, axis=-1, keepdims=True)
    mixed = rstd * rstd * rstd * (total / D)
    for k in range(NK):
        for r in range(2):
            lo = k * CW + r * HW
            v = max(0, min(HW, D - lo))
            if v:
                dtok_ref[:, lo : lo + v] = (
                    rstd * dn[2 * k + r, :, 0:v] - tf[:, lo : lo + v] * mixed
                ).astype(BF)

    for cp in stores[-2:]:
        cp.wait()
    for cp in sends:
        cp.wait_send()


def n_sends():
    early = sum(EARLY)
    late = NK - early
    n = early + (1 if early else 0)
    n += 7 * (late + 2 * early) + 7 * (2 if early else 1)
    n += 7 * (late + 2 * early) + 2 * late + 4 * NK
    n += NK + 2 * late + 7 * (late + 2 * early) + 7 * (late + 2 * early) + early
    return n


def local(tokens, norm_gain, expert_ids, combine_weight, cotangent, w_gate, w_up, w_down):
    vm = pl.BlockSpec(memory_space=pltpu.VMEM)
    hbm = pl.BlockSpec(memory_space=pl.ANY)
    dma = pltpu.SemaphoreType.DMA
    scratch = [
        pltpu.VMEM((FQ, D), BF), pltpu.VMEM((FQ, D), BF), pltpu.VMEM((FQ, D), BF),
        pltpu.VMEM((NK, 2, 2, TOK, CW), BF),
        pltpu.VMEM((2, 8, 256), F32), pltpu.VMEM((2, 8, 8, 256), F32),
        pltpu.VMEM((NK, 2, 256, CW), BF),
        pltpu.VMEM((NK, 2, ROWS, 8, CW), BF),
        pltpu.VMEM((NK, 2, TOTAL // 8, 8, CW), BF),
        pltpu.VMEM((8 * ROWS, 256), F32), pltpu.VMEM((2, 8 * ROWS, 256), BF),
        pltpu.VMEM((2, 8 * ROWS, 128), F32),
        pltpu.VMEM((TOTAL, FQ), F32), pltpu.VMEM((TOTAL, FQ), F32), pltpu.VMEM((TOTAL, FQ), F32),
        pltpu.VMEM((TOTAL, FQ), BF), pltpu.VMEM((TOTAL, FQ), BF),
        pltpu.VMEM((FQ, TOTAL), BF), pltpu.VMEM((FQ, TOTAL), BF), pltpu.VMEM((FQ, TOTAL), BF),
        pltpu.VMEM((NK, 2, TOTAL, HW), BF),
        pltpu.VMEM((NK, TOTAL, HW), BF),
        pltpu.VMEM((NK, TOTAL // 8, 8, HW), BF),
        pltpu.VMEM((NK, BLK // 4, 8, HW), BF), pltpu.VMEM((NK, BLK // 4, 8, HW), BF),
        pltpu.VMEM((NK, 2, ROWS, 8, HW), BF), pltpu.VMEM((NK, 2, 256, HW), BF),
        pltpu.VMEM((NK, 2, 8, TOK, HW), BF),
        pltpu.VMEM((NK, 2, TOK, HW), BF), pltpu.VMEM((NK, 2, TOK, HW), BF),
        pltpu.VMEM((2 * NK, TOK, HW), F32),
        pltpu.VMEM((2, GB, D), BF),
        dma((3,)), dma((1,)), dma((2, 8)), dma((1,)), dma((NK + 1,)), dma((1,)), dma((NK, 2, 8)),
        dma((NK, 2, 2, 4)), dma((NK, 2)), dma((NK, 4)), dma((NK,)), dma((NK, 2)), dma((NK, 2, 8)),
        dma((NK, 2, 8)), dma((NK,)), dma((n_sends(),)), dma((3 * NG,)),
    ]
    d_tokens, grad_gate, grad_up, grad_down = pl.pallas_call(
        kernel,
        out_shape=(
            jax.ShapeDtypeStruct((TOK, D), BF),
            jax.ShapeDtypeStruct((1, FQ, D), BF),
            jax.ShapeDtypeStruct((1, FQ, D), BF),
            jax.ShapeDtypeStruct((1, FQ, D), BF),
        ),
        in_specs=[vm, vm, vm, vm, vm, hbm, hbm, hbm],
        out_specs=(vm, hbm, hbm, hbm),
        scratch_shapes=scratch,
        compiler_params=pltpu.CompilerParams(
            collective_id=0, has_side_effects=True, vmem_limit_bytes=63 << 20
        ),
    )(
        tokens, norm_gain, expert_ids.T, combine_weight.T, cotangent,
        jnp.swapaxes(w_gate, 1, 2), jnp.swapaxes(w_up, 1, 2), w_down,
    )
    return d_tokens, jnp.swapaxes(grad_gate, 1, 2), jnp.swapaxes(grad_up, 1, 2), grad_down


def solution(mesh):
    placed = (
        P("sq", None),
        P(),
        P("sq", None),
        P("sq", None),
        P("sq", None),
        P("sq", None, None),
        P("sq", None, None),
        P("sq", None, None),
    )
    return jax.shard_map(
        local,
        mesh=mesh,
        in_specs=placed,
        out_specs=(P("sq", None), P("sq", None, None), P("sq", None, None), P("sq", None, None)),
        check_vma=False,
    )
```

time: 309 us -> 133 us (0.43)
  waiting for transfers between devices: 178 us -> 0 us
  Pallas kernels: 0 us -> 122 us
  matrix products: 54.5 us -> 0 us
  starting transfers between devices: 28.7 us -> 0 us
  local copies, waits for them, and re-layouts: 38.1 us -> 11 us
  other arithmetic: 7.43 us -> 0.01 us
    all_to_all x3 -> x0, waiting for transfers between devices: 178 us -> none  [the longest x1 71.4 us: local(): lax.all_to_all(spread(send_x), 'sq', split_axis=0, concat_axis=0, tiled=T...]
    pallas_call x0 -> x1, Pallas kernels: none -> 122 us  [local(): pl.pallas_call(kernel, out_shape=(jax.ShapeDtypeStruct((TOK, D), BF), jax...]
    dot_general x12 -> x0, matrix products: 54.5 us -> none  [the longest x3 20.6 us: contract_cols(): lax.dot_general(left, right, (((1,), (1,)), ((), ())), preferred_element_...]
    all_to_all x3 -> x0, starting transfers between devices: 28.7 us -> none  [the longest x1 11.9 us: local(): lax.all_to_all(spread(send_x), 'sq', split_axis=0, concat_axis=0, tiled=T...]
    reshape x4 -> x0, local copies, waits for them, and re-layouts: 24 us -> none  [the longest x1 8.02 us: local(): dy_e = got_dy.reshape(rows_total, width)]
    unnamed x27 -> x10, local copies, waits for them, and re-layouts: 0.84 us -> 11 us
    broadcast_in_dim x4 -> x0, local copies, waits for them, and re-layouts: 6.84 us -> none  [spread(): jnp.broadcast_to(shaped, (expert_count, QUARTERS, slot_count, width))]
    convert_element_type x3 -> x0, local copies, waits for them, and re-layouts: 6.34 us -> none  [the longest x1 6.16 us: local(): (contract_cols(d_gate, gate_w) + contract_cols(d_up, up_w)).astype(jnp.bf...]
  transfers between devices with their start and end apart: 3 -> 0, of which waited for: 3 -> 0; matrix products, arithmetic and copies ran while one was open for 13% -> 0% of each run, Pallas kernels for 0% -> 0%
where the time goes in v1:
time: 133 us
  Pallas kernels  122 us (92%)
  local copies, waits for them, and re-layouts  11 us (8%)
    pallas_call x1, Pallas kernels, local(): pl.pallas_call(kernel, out_shape=(jax.ShapeDtypeStruct((TOK, D), BF), jax...  122 us
    unnamed x10, local copies, waits for them, and re-layouts  11 us

profile of v1, /device:TPU:1, one launch (start us, length us, event | category | flops | bytes accessed | tf_op | source)
XLA Modules:
  0.0 133.3 jit_solution(6013729976942305769)
XLA Ops:
  0.6 121.6 %shard_map.111 = (bf16[32,2880]{1,0:T(8,128)(2,1)}, bf16[1,720,2880]{2,1,0:T(8,128)(2,1)}, bf16[1,720,2880]{2,1,0:T(8,128)(2,1)}, bf16[1,720,2880]{2,1,0:T(8,128)(2,1)}) custom-call(bf16[32,2880]{1,0:T(8,128)(2,1)} %tok_ref.1, f32[2880]{0:T(1024)} %gain_ref.1, s32[4,32]{1,0:T(4,128)} %bitcast.12, f32[4,32]{1,0:T(4,128)} %bitcast.13, ...), custom_call_target="tpu_custom_call" | custom-call | tf_op jit(solution)/shard_map/pallas_call | solution.py:535
  122.2 1.6 %copy.16 = bf16[32,2880]{1,0:T(8,128)(2,1)} copy(bf16[32,2880]{1,0:T(8,128)(2,1)} %get-tuple-element.16) | data formatting | bytes 368640
  123.9 0.0 copy-start
  123.9 0.0 slice-start
  123.9 4.8 %copy.17 = bf16[1,2880,720]{1,2,0:T(8,128)(2,1)} copy(bf16[1,2880,720]{1,2,0:T(8,128)(2,1)} %bitcast.11) | data formatting | bytes 8294400
  128.7 0.0 copy-done
  128.7 0.0 slice-start.1
  128.7 2.0 %copy.18 = bf16[1,2880,720]{1,2,0:T(8,128)(2,1)} copy(bf16[1,2880,720]{1,2,0:T(8,128)(2,1)S(1)} %bitcast.10) | data formatting | bytes 8294400
  130.7 0.6 slice-done
  131.3 0.0 slice-done.1
  131.3 2.0 %copy.19 = bf16[1,720,2880]{2,1,0:T(8,128)(2,1)} copy(bf16[1,720,2880]{2,1,0:T(8,128)(2,1)S(1)} %bitcast.9) | data formatting | bytes 8294400
  (1 shorter events, 0.0 us)
Async XLA Ops:
  123.9 4.8 %copy-start = (bf16[1,720,2880]{2,1,0:T(8,128)(2,1)S(1)}, bf16[1,720,2880]{2,1,0:T(8,128)(2,1)}, u32[]{:S(2)}) copy-start(bf16[1,720,2880]{2,1,0:T(8,128)(2,1)} %get-tuple-element.10) | copy-start | bytes 12441604
  123.9 7.4 %slice-start = ((s8[4239360]{0:T(1024)(128)(4,1)}), s8[4194304]{0:T(1024)(128)(4,1)S(1)}, s32[]{:S(2)}) async-start(s8[4239360]{0:T(1024)(128)(4,1)} %bitcast.8), calls=%async_computation | async-start | bytes 8388608
  128.7 2.6 %slice-start.1 = ((s8[4239360]{0:T(1024)(128)(4,1)}), s8[45056]{0:T(1024)(128)(4,1)S(1)}, s32[]{:S(2)}) async-start(s8[4239360]{0:T(1024)(128)(4,1)} %bitcast.8), calls=%async_computation.1 | async-start | bytes 90112

commit v2 on v1

--- a/solution.py
+++ b/solution.py
@@ -19,12 +19,13 @@
 TOK = 32
 TOP = 4
 SLOTS = 5
-CW = 768
+CW = 512
 HW = CW // 2
 NK = -(-D // CW)
 VALID = [min(CW, D - k * CW) for k in range(NK)]
 LANES = [-(-v // 128) * 128 for v in VALID]
-EARLY = [False, False, False, False]
+EARLY = [False, False, False, True, True, False]
+WINDOW = 2
 ROWS = 8 * SLOTS
 BLK = 4 * ROWS
 TOTAL = 4 * BLK
@@ -50,11 +51,11 @@
 
 def kernel(
     tok_ref, gain_ref, ids_ref, cw_ref, cot_ref, wg_hbm, wu_hbm, wd_hbm,
-    dtok_ref, gg_hbm, gu_hbm, gd_hbm,
-    wg, wu, wd, own, meta_own, meta_got, gath, rows, xd, sel_f, sel, scale, up_a, gate_a, dhid_a,
-    dg, du, dg_t, du_t, hid_t, part, part_got, psum, h_got, drow, z_got, tsum, x_got, f_out, f_got, dn, gs,
+    dtok_ref, gg_ref, gu_ref, gd_ref,
+    own, meta_own, meta_got, gath, rows, xd, sel_f, sel, scale, up_a, gate_a, dhid_a,
+    dg, du, dg_t, du_t, hid_t, part, part_got, psum, h_got, drow, z_got, tsum, x_got, f_out, f_got, dn,
     wsem, psem, msem, msend, fsem, hsem, xsem, zsem, ysem, csem, rcsem, rhsem, rzsem, rxsem, rfsem,
-    send, gsem,
+    send,
 ):
     me = lax.axis_index("sq")
     c = lax.rem(me, 2)
@@ -67,6 +68,7 @@
     yl = 3 - y
     any_early = any(EARLY)
 
+    wg, wu, wd = gg_ref.at[0], gu_ref.at[0], gd_ref.at[0]
     weights = [
         pltpu.make_async_copy(wg_hbm.at[0], wg, wsem.at[0]),
         pltpu.make_async_copy(wu_hbm.at[0], wu, wsem.at[1]),
@@ -188,19 +190,14 @@
                 meta_own.at[hh], meta_got.at[hh, src_mine], msem.at[i, src_mine]
             ).start()
 
-    late = [k for k in range(NK) if not EARLY[k]]
-    order = list(range(NK))
-    if not any_early:
+    if EARLY[0] or not any_early:
         send_meta()
-        for k in order:
-            send_x(k)
+        send_x(0)
     else:
-        for k in late[:1]:
-            send_x(k)
+        send_x(0)
         send_meta()
-        for k in order:
-            if k not in late[:1]:
-                send_x(k)
+    for k in range(1, WINDOW):
+        send_x(k)
 
     def build():
         e_of = lax.broadcasted_iota(jnp.int32, (8, 256), 0).astype(F32) + (8 * x).astype(F32)
@@ -240,6 +237,8 @@
         for i, hh in enumerate(hs):
             for s in range(8):
                 arrived(gath.at[k, hh, pl.ds(TOK * s, TOK), pl.ds(0, n)], xsem.at[k, i, s])
+        if k + WINDOW < NK:
+            send_x(k + WINDOW)
         for i, hh in enumerate(hs):
             picked = dot(sel[hh], gath[k, hh, :, 0:n])
             picked = (picked * scale[hh, :, 0:1]).astype(BF)
@@ -421,26 +420,16 @@
             for r in range(2):
                 dn[2 * k + r] = dn[2 * k + r] + f_got[k, r].astype(F32)
 
-    stores = []
-
     def grad(which, b):
-        slot = len(stores) % 2
-        if len(stores) >= 2:
-            stores[-2].wait()
         left = (dg_t, du_t, hid_t)[which]
+        out = (wg, wu, wd)[which]
         for k in range(NK):
             lo, v = k * CW, VALID[k]
-            gs[slot, :, lo : lo + v] = dot(
+            out[b * GB : (b + 1) * GB, lo : lo + v] = dot(
                 left[b * GB : (b + 1) * GB, :], flat(xd, k, which // 2)[:, 0:v]
             ).astype(BF)
-        cp = pltpu.make_async_copy(
-            gs.at[slot], (gg_hbm, gu_hbm, gd_hbm)[which].at[0, pl.ds(b * GB, GB), :],
-            gsem.at[len(stores)],
-        )
-        cp.start()
-        stores.append(cp)
-
-    fill = [lambda w=w, b=b: grad(w, b) for w in range(3) for b in range(NG)]
+
+    fill = [lambda w=w, b=b: grad(w, b) for w in (2, 0, 1) for b in range(NG)]
 
     def filler():
         if fill:
@@ -457,7 +446,7 @@
             back_core(step - 1)
         if 0 <= step - 2 < NK:
             back_pair(step - 2)
-        if step >= 2:
+        if step >= 2 and (len(fill) > 2 * NG or step >= NK - 1):
             filler()
         if 0 <= step - 3 < NK:
             back_token(step - 3)
@@ -487,8 +476,6 @@
                     rstd * dn[2 * k + r, :, 0:v] - tf[:, lo : lo + v] * mixed
                 ).astype(BF)
 
-    for cp in stores[-2:]:
-        cp.wait()
     for cp in sends:
         cp.wait_send()
 
@@ -503,12 +490,22 @@
     return n
 
 
+def write_out(a, b, c, a_hbm, b_hbm, c_hbm, sem):
+    copies = [
+        pltpu.make_async_copy(src, dst, sem.at[i])
+        for i, (src, dst) in enumerate(((a, a_hbm), (b, b_hbm), (c, c_hbm)))
+    ]
+    for cp in copies:
+        cp.start()
+    for cp in copies:
+        cp.wait()
+
+
 def local(tokens, norm_gain, expert_ids, combine_weight, cotangent, w_gate, w_up, w_down):
     vm = pl.BlockSpec(memory_space=pltpu.VMEM)
     hbm = pl.BlockSpec(memory_space=pl.ANY)
     dma = pltpu.SemaphoreType.DMA
     scratch = [
-        pltpu.VMEM((FQ, D), BF), pltpu.VMEM((FQ, D), BF), pltpu.VMEM((FQ, D), BF),
         pltpu.VMEM((NK, 2, 2, TOK, CW), BF),
         pltpu.VMEM((2, 8, 256), F32), pltpu.VMEM((2, 8, 8, 256), F32),
         pltpu.VMEM((NK, 2, 256, CW), BF),
@@ -527,29 +524,36 @@
         pltpu.VMEM((NK, 2, 8, TOK, HW), BF),
         pltpu.VMEM((NK, 2, TOK, HW), BF), pltpu.VMEM((NK, 2, TOK, HW), BF),
         pltpu.VMEM((2 * NK, TOK, HW), F32),
-        pltpu.VMEM((2, GB, D), BF),
         dma((3,)), dma((1,)), dma((2, 8)), dma((1,)), dma((NK + 1,)), dma((1,)), dma((NK, 2, 8)),
         dma((NK, 2, 2, 4)), dma((NK, 2)), dma((NK, 4)), dma((NK,)), dma((NK, 2)), dma((NK, 2, 8)),
-        dma((NK, 2, 8)), dma((NK,)), dma((n_sends(),)), dma((3 * NG,)),
+        dma((NK, 2, 8)), dma((NK,)), dma((n_sends(),)),
     ]
     d_tokens, grad_gate, grad_up, grad_down = pl.pallas_call(
         kernel,
         out_shape=(
             jax.ShapeDtypeStruct((TOK, D), BF),
-            jax.ShapeDtypeStruct((1, FQ, D), BF),
-            jax.ShapeDtypeStruct((1, FQ, D), BF),
-            jax.ShapeDtypeStruct((1, FQ, D), BF),
+            pltpu.VMEM((1, FQ, D), BF),
+            pltpu.VMEM((1, FQ, D), BF),
+            pltpu.VMEM((1, FQ, D), BF),
         ),
         in_specs=[vm, vm, vm, vm, vm, hbm, hbm, hbm],
-        out_specs=(vm, hbm, hbm, hbm),
+        out_specs=(vm, vm, vm, vm),
         scratch_shapes=scratch,
         compiler_params=pltpu.CompilerParams(
-            collective_id=0, has_side_effects=True, vmem_limit_bytes=63 << 20
+            collective_id=0, has_side_effects=True, vmem_limit_bytes=48 << 20
         ),
     )(
         tokens, norm_gain, expert_ids.T, combine_weight.T, cotangent,
         jnp.swapaxes(w_gate, 1, 2), jnp.swapaxes(w_up, 1, 2), w_down,
     )
+    grad_gate, grad_up, grad_down = pl.pallas_call(
+        write_out,
+        out_shape=(jax.ShapeDtypeStruct((1, FQ, D), BF),) * 3,
+        in_specs=[vm] * 3,
+        out_specs=(hbm,) * 3,
+        scratch_shapes=[dma((3,))],
+        compiler_params=pltpu.CompilerParams(has_side_effects=True, vmem_limit_bytes=1 << 20),
+    )(grad_gate, grad_up, grad_down)
     return d_tokens, jnp.swapaxes(grad_gate, 1, 2), jnp.swapaxes(grad_up, 1, 2), grad_down
 
 

time: 133 us -> 120 us (0.902)
  local copies, waits for them, and re-layouts: 11 us -> 0.68 us
  Pallas kernels: 122 us -> 119 us
    unnamed x10 -> x3, local copies, waits for them, and re-layouts: 11 us -> 0.68 us
    pallas_call x1 -> x2, Pallas kernels: 122 us -> 119 us  [the longest x1 114 us: local(): pl.pallas_call(kernel, out_shape=(jax.ShapeDtypeStruct((TOK, D), BF), plt...]
where the time goes in v2:
time: 120 us
  Pallas kernels  119 us (99%)
    pallas_call x1, Pallas kernels, local(): pl.pallas_call(kernel, out_shape=(jax.ShapeDtypeStruct((TOK, D), BF), plt...  114 us
    pallas_call x1, Pallas kernels, local(): pl.pallas_call(write_out, out_shape=(jax.ShapeDtypeStruct((1, FQ, D), BF)...  4.73 us

profile of v2, /device:TPU:1, one launch (start us, length us, event | category | flops | bytes accessed | tf_op | source)
XLA Modules:
  0.0 119.9 jit_solution(11125503605343441997)
XLA Ops:
  0.6 113.8 %shard_map.111 = (bf16[32,2880]{1,0:T(8,128)(2,1)}, bf16[1,720,2880]{2,1,0:T(8,128)(2,1)S(1)}, bf16[1,720,2880]{2,1,0:T(8,128)(2,1)S(1)}, bf16[1,720,2880]{2,1,0:T(8,128)(2,1)S(1)}) custom-call(bf16[32,2880]{1,0:T(8,128)(2,1)} %tok_ref.1, f32[2880]{0:T(1024)} %gain_ref.1, s32[4,32]{1,0:T(4,128)} %bitcast.8, f32[4,32]{1,0:T(4,128)} %bitcast.9, ...), custom_call_target="tpu_custom_call" | custom-call | tf_op jit(solution)/shard_map/pallas_call | solution.py:531
  114.5 0.0 copy-start
  114.5 4.7 %shard_map.112 = (bf16[1,720,2880]{2,1,0:T(8,128)(2,1)}, bf16[1,720,2880]{2,1,0:T(8,128)(2,1)}, bf16[1,720,2880]{2,1,0:T(8,128)(2,1)}) custom-call(bf16[1,720,2880]{2,1,0:T(8,128)(2,1)S(1)} %get-tuple-element.12.a, bf16[1,720,2880]{2,1,0:T(8,128)(2,1)S(1)} %get-tuple-element.13.b, bf16[1,720,2880]{2,1,0:T(8,128)(2,1)S(1)} %get-tuple-element.14.c), custom_call_target="tpu_custom_call" | custom-call | tf_op jit(solution)/shard_map/pallas_call | solution.py:549
  119.2 0.0 copy-done
  119.2 0.7 copy.13
Async XLA Ops:
  114.5 4.7 %copy-start = (bf16[32,2880]{1,0:T(8,128)(2,1)S(1)}, bf16[32,2880]{1,0:T(8,128)(2,1)}, u32[]{:S(2)}) copy-start(bf16[32,2880]{1,0:T(8,128)(2,1)} %get-tuple-element.22) | copy-start | bytes 552964

commit v3 on v2

--- a/solution.py
+++ b/solution.py
@@ -25,7 +25,9 @@
 VALID = [min(CW, D - k * CW) for k in range(NK)]
 LANES = [-(-v // 128) * 128 for v in VALID]
 EARLY = [False, False, False, True, True, False]
-WINDOW = 2
+WINDOW = 3
+AHEAD = (1, 3, 4)
+BACK = (1, 3, 5, 7, 8)
 ROWS = 8 * SLOTS
 BLK = 4 * ROWS
 TOTAL = 4 * BLK
@@ -50,11 +52,11 @@
 
 
 def kernel(
-    tok_ref, gain_ref, ids_ref, cw_ref, cot_ref, wg_hbm, wu_hbm, wd_hbm,
+    tok_hbm, gain_hbm, ids_hbm, cw_hbm, cot_hbm, wg_hbm, wu_hbm, wd_hbm,
     dtok_ref, gg_ref, gu_ref, gd_ref,
-    own, meta_own, meta_got, gath, rows, xd, sel_f, sel, scale, up_a, gate_a, dhid_a,
+    tok_ref, gain_ref, ids_ref, cw_ref, cot_ref, own, meta_own, meta_got, gath, rows, xd, sel_f, sel, scale, up_a, gate_a, dhid_a,
     dg, du, dg_t, du_t, hid_t, part, part_got, psum, h_got, drow, z_got, tsum, x_got, f_out, f_got, dn,
-    wsem, psem, msem, msend, fsem, hsem, xsem, zsem, ysem, csem, rcsem, rhsem, rzsem, rxsem, rfsem,
+    wsem, isem, msem, msend, fsem, hsem, xsem, zsem, ysem, csem, rcsem, rhsem, rzsem, rxsem, rfsem,
     send,
 ):
     me = lax.axis_index("sq")
@@ -74,8 +76,17 @@
         pltpu.make_async_copy(wu_hbm.at[0], wu, wsem.at[1]),
         pltpu.make_async_copy(wd_hbm.at[0], wd, wsem.at[2]),
     ]
-    for w in weights:
-        w.start()
+    inputs = [
+        pltpu.make_async_copy(src, dst, isem.at[i])
+        for i, (src, dst) in enumerate(
+            (
+                (tok_hbm, tok_ref), (gain_hbm, gain_ref), (ids_hbm, ids_ref),
+                (cw_hbm, cw_ref), (cot_hbm, cot_ref),
+            )
+        )
+    ]
+    for cp in inputs:
+        cp.start()
 
     peers_x = [(dx, dr) for dx in range(4) for dr in range(2) if (dx, dr) != (0, 0)]
     peers_z = [(dz, pr) for dz in range(4) for pr in range(2) if (dz, pr) != (0, 0)]
@@ -97,6 +108,9 @@
 
     def gain(lo, v):
         return gain_ref[pl.ds(lo, v)].reshape(1, v)
+
+    for cp in inputs:
+        cp.wait()
 
     tf = tok_ref[...].astype(F32)
     rstd = lax.rsqrt(jnp.mean(tf * tf, axis=-1, keepdims=True) + eps)
@@ -198,6 +212,9 @@
         send_meta()
     for k in range(1, WINDOW):
         send_x(k)
+
+    for w in weights:
+        w.start()
 
     def build():
         e_of = lax.broadcasted_iota(jnp.int32, (8, 256), 0).astype(F32) + (8 * x).astype(F32)
@@ -302,15 +319,12 @@
         dhid_a[...] = dhid if k == 0 else dhid_a[...] + dhid
 
     build()
-    for step in range(NK + 3):
+    for step in range(NK + AHEAD[2]):
         if step < NK:
             select(step)
-        if 0 <= step - 1 < NK:
-            forward(step - 1)
-        if 0 <= step - 2 < NK:
-            finish(step - 2)
-        if 0 <= step - 3 < NK:
-            up_matmuls(step - 3)
+        for stage, after in zip((forward, finish, up_matmuls), AHEAD, strict=True):
+            if 0 <= step - after < NK:
+                stage(step - after)
 
     def pointwise(i, carry):
         b = pl.ds(pl.multiple_of(i * BLK, BLK), BLK)
@@ -431,31 +445,20 @@
 
     fill = [lambda w=w, b=b: grad(w, b) for w in (2, 0, 1) for b in range(NG)]
 
-    def filler():
-        if fill:
-            fill.pop(0)()
-
-    for step in range(NK + 5):
+    for step in range(NK + BACK[-1]):
         if step < NK:
             partial(step)
         if step == 0:
             hid_t[...] = gate_a[...].T.astype(BF)
             dg_t[...] = dg[...].T
             du_t[...] = du[...].T
-        if 0 <= step - 1 < NK:
-            back_core(step - 1)
-        if 0 <= step - 2 < NK:
-            back_pair(step - 2)
-        if step >= 2 and (len(fill) > 2 * NG or step >= NK - 1):
-            filler()
-        if 0 <= step - 3 < NK:
-            back_token(step - 3)
-        if 0 <= step - 4 < NK:
-            back_x(step - 4)
-        if 0 <= step - 5 < NK:
-            back_last(step - 5)
+        for i, stage in enumerate((back_core, back_pair, back_token, back_x, back_last)):
+            if 0 <= step - BACK[i] < NK:
+                stage(step - BACK[i])
+            if i == 1 and step >= 2 and (len(fill) > 2 * NG or step >= NK - 1) and fill:
+                fill.pop(0)()
     while fill:
-        filler()
+        fill.pop(0)()
 
     total = jnp.zeros((TOK, 1), F32)
     for k in range(NK):
@@ -490,10 +493,10 @@
     return n
 
 
-def write_out(a, b, c, a_hbm, b_hbm, c_hbm, sem):
+def write_out(t, a, b, c, t_hbm, a_hbm, b_hbm, c_hbm, sem):
     copies = [
         pltpu.make_async_copy(src, dst, sem.at[i])
-        for i, (src, dst) in enumerate(((a, a_hbm), (b, b_hbm), (c, c_hbm)))
+        for i, (src, dst) in enumerate(((t, t_hbm), (a, a_hbm), (b, b_hbm), (c, c_hbm)))
     ]
     for cp in copies:
         cp.start()
@@ -506,6 +509,8 @@
     hbm = pl.BlockSpec(memory_space=pl.ANY)
     dma = pltpu.SemaphoreType.DMA
     scratch = [
+        pltpu.VMEM((TOK, D), BF), pltpu.VMEM((D,), F32), pltpu.VMEM((TOP, TOK), jnp.int32),
+        pltpu.VMEM((TOP, TOK), F32), pltpu.VMEM((TOK, D), BF),
         pltpu.VMEM((NK, 2, 2, TOK, CW), BF),
         pltpu.VMEM((2, 8, 256), F32), pltpu.VMEM((2, 8, 8, 256), F32),
         pltpu.VMEM((NK, 2, 256, CW), BF),
@@ -524,19 +529,19 @@
         pltpu.VMEM((NK, 2, 8, TOK, HW), BF),
         pltpu.VMEM((NK, 2, TOK, HW), BF), pltpu.VMEM((NK, 2, TOK, HW), BF),
         pltpu.VMEM((2 * NK, TOK, HW), F32),
-        dma((3,)), dma((1,)), dma((2, 8)), dma((1,)), dma((NK + 1,)), dma((1,)), dma((NK, 2, 8)),
+        dma((3,)), dma((5,)), dma((2, 8)), dma((1,)), dma((NK + 1,)), dma((1,)), dma((NK, 2, 8)),
         dma((NK, 2, 2, 4)), dma((NK, 2)), dma((NK, 4)), dma((NK,)), dma((NK, 2)), dma((NK, 2, 8)),
         dma((NK, 2, 8)), dma((NK,)), dma((n_sends(),)),
     ]
     d_tokens, grad_gate, grad_up, grad_down = pl.pallas_call(
         kernel,
         out_shape=(
-            jax.ShapeDtypeStruct((TOK, D), BF),
+            pltpu.VMEM((TOK, D), BF),
             pltpu.VMEM((1, FQ, D), BF),
             pltpu.VMEM((1, FQ, D), BF),
             pltpu.VMEM((1, FQ, D), BF),
         ),
-        in_specs=[vm, vm, vm, vm, vm, hbm, hbm, hbm],
+        in_specs=[hbm] * 8,
         out_specs=(vm, vm, vm, vm),
         scratch_shapes=scratch,
         compiler_params=pltpu.CompilerParams(
@@ -546,14 +551,15 @@
         tokens, norm_gain, expert_ids.T, combine_weight.T, cotangent,
         jnp.swapaxes(w_gate, 1, 2), jnp.swapaxes(w_up, 1, 2), w_down,
     )
-    grad_gate, grad_up, grad_down = pl.pallas_call(
+    d_tokens, grad_gate, grad_up, grad_down = pl.pallas_call(
         write_out,
-        out_shape=(jax.ShapeDtypeStruct((1, FQ, D), BF),) * 3,
-        in_specs=[vm] * 3,
-        out_specs=(hbm,) * 3,
-        scratch_shapes=[dma((3,))],
+        out_shape=(jax.ShapeDtypeStruct((TOK, D), BF),)
+        + (jax.ShapeDtypeStruct((1, FQ, D), BF),) * 3,
+        in_specs=[vm] * 4,
+        out_specs=(hbm,) * 4,
+        scratch_shapes=[dma((4,))],
         compiler_params=pltpu.CompilerParams(has_side_effects=True, vmem_limit_bytes=1 << 20),
-    )(grad_gate, grad_up, grad_down)
+    )(d_tokens, grad_gate, grad_up, grad_down)
     return d_tokens, jnp.swapaxes(grad_gate, 1, 2), jnp.swapaxes(grad_up, 1, 2), grad_down
 
 

time: 120 us -> 111 us (0.925)
  Pallas kernels: 119 us -> 110 us
    pallas_call x2, Pallas kernels: 119 us -> 110 us  [the longest x1 105 us: local(): pl.pallas_call(kernel, out_shape=(pltpu.VMEM((TOK, D), BF), pltpu.VMEM((1...]
where the time goes in v3:
time: 111 us; the launch traced here: 110 us
  Pallas kernels  110 us (99%)
    pallas_call x1, Pallas kernels, local(): pl.pallas_call(kernel, out_shape=(pltpu.VMEM((TOK, D), BF), pltpu.VMEM((1...  105 us
    pallas_call x1, Pallas kernels, local(): pl.pallas_call(write_out, out_shape=(jax.ShapeDtypeStruct((TOK, D), BF),)...  4.8 us

profile of v3, /device:TPU:1, one launch (start us, length us, event | category | flops | bytes accessed | tf_op | source)
XLA Modules:
  0.0 110.5 jit_solution(3399981699675120807)
XLA Ops:
  0.6 104.8 %shard_map.111 = (bf16[32,2880]{1,0:T(8,128)(2,1)S(1)}, bf16[1,720,2880]{2,1,0:T(8,128)(2,1)S(1)}, bf16[1,720,2880]{2,1,0:T(8,128)(2,1)S(1)}, bf16[1,720,2880]{2,1,0:T(8,128)(2,1)S(1)}) custom-call(bf16[32,2880]{1,0:T(8,128)(2,1)} %tok_hbm.1, f32[2880]{0:T(1024)} %gain_hbm.1, s32[4,32]{1,0:T(4,128)} %bitcast.8, f32[4,32]{1,0:T(4,128)} %bitcast.9, ...), custom_call_target="tpu_custom_call" | custom-call | tf_op jit(solution)/shard_map/pallas_call | solution.py:536
  105.5 4.8 %shard_map.112 = (bf16[32,2880]{1,0:T(8,128)(2,1)}, bf16[1,720,2880]{2,1,0:T(8,128)(2,1)}, bf16[1,720,2880]{2,1,0:T(8,128)(2,1)}, bf16[1,720,2880]{2,1,0:T(8,128)(2,1)}) custom-call(bf16[32,2880]{1,0:T(8,128)(2,1)S(1)} %get-tuple-element.12.t, bf16[1,720,2880]{2,1,0:T(8,128)(2,1)S(1)} %get-tuple-element.13.a, bf16[1,720,2880]{2,1,0:T(8,128)(2,1)S(1)} %get-tuple-element.14.b, ...), custom_call_target="tpu_custom_call" | custom-call | tf_op jit(solution)/shard_map/pallas_call | solution.py:554

commit v4 on v3

--- a/solution.py
+++ b/solution.py
@@ -27,7 +27,7 @@
 EARLY = [False, False, False, True, True, False]
 WINDOW = 3
 AHEAD = (1, 3, 4)
-BACK = (1, 3, 5, 7, 8)
+BACK = (1, 4, 6, 8, 9)
 ROWS = 8 * SLOTS
 BLK = 4 * ROWS
 TOTAL = 4 * BLK

time: 111 us -> 112 us (level)
  no operation moved by 1% of the time
where the time goes in v4:
time: 112 us; the launch traced here: 111 us
  Pallas kernels  111 us (99%)
    pallas_call x1, Pallas kernels, local(): pl.pallas_call(kernel, out_shape=(pltpu.VMEM((TOK, D), BF), pltpu.VMEM((1...  106 us
    pallas_call x1, Pallas kernels, local(): pl.pallas_call(write_out, out_shape=(jax.ShapeDtypeStruct((TOK, D), BF),)...  4.8 us

profile of v4, /device:TPU:1, one launch (start us, length us, event | category | flops | bytes accessed | tf_op | source)
XLA Modules:
  0.0 111.4 jit_solution(8681103548713906930)
XLA Ops:
  0.6 105.8 %shard_map.111 = (bf16[32,2880]{1,0:T(8,128)(2,1)S(1)}, bf16[1,720,2880]{2,1,0:T(8,128)(2,1)S(1)}, bf16[1,720,2880]{2,1,0:T(8,128)(2,1)S(1)}, bf16[1,720,2880]{2,1,0:T(8,128)(2,1)S(1)}) custom-call(bf16[32,2880]{1,0:T(8,128)(2,1)} %tok_hbm.1, f32[2880]{0:T(1024)} %gain_hbm.1, s32[4,32]{1,0:T(4,128)} %bitcast.8, f32[4,32]{1,0:T(4,128)} %bitcast.9, ...), custom_call_target="tpu_custom_call" | custom-call | tf_op jit(solution)/shard_map/pallas_call | solution.py:536
  106.5 4.8 %shard_map.112 = (bf16[32,2880]{1,0:T(8,128)(2,1)}, bf16[1,720,2880]{2,1,0:T(8,128)(2,1)}, bf16[1,720,2880]{2,1,0:T(8,128)(2,1)}, bf16[1,720,2880]{2,1,0:T(8,128)(2,1)}) custom-call(bf16[32,2880]{1,0:T(8,128)(2,1)S(1)} %get-tuple-element.12.t, bf16[1,720,2880]{2,1,0:T(8,128)(2,1)S(1)} %get-tuple-element.13.a, bf16[1,720,2880]{2,1,0:T(8,128)(2,1)S(1)} %get-tuple-element.14.b, ...), custom_call_target="tpu_custom_call" | custom-call | tf_op jit(solution)/shard_map/pallas_call | solution.py:554
